TPU v7x, 32 devices: a whole 2x2x4 slice. The times are simulated.
32 devices in a mesh: groups: 2 (over y), tensor: 4 (over z), adapter: 4 (over x, core).
Axes of the slice: x: 2, y: 2, z: 4, core: 2. Of those that a mesh axis runs over, the one named last changes fastest.
Arguments:
- attended: bfloat16 [8, 64, 8192], P(('groups', 'adapter'), None, 'tensor'), parts along dimension 0, may hold values from -6 to 6
- out_weight: bfloat16 [8192, 8192], P('tensor'), may hold values from -0.0625 to 0.0625
- adapter_ids: int32 [8, 64], P(('groups', 'adapter')), parts along dimension 0, may hold values from 0 to 127, as said below
- shrink_weight: bfloat16 [128, 8192, 64], P('adapter', 'tensor'), may hold values from -0.0625 to 0.0625
- expand_weight: bfloat16 [128, 64, 8192], P('adapter', None, 'tensor'), may hold values from -0.75 to 0.75
Outputs:
- projected: bfloat16 [8, 64, 8192], P(('groups', 'adapter'), 'tensor'), parts along dimension 0
There are 2 independent parts, one for each index of `groups`. A program takes and returns all parts, laid end to end along the dimension named above; an argument that names none is the same for every part. Nothing has to cross between parts.
Inputs may be any that keep to these rules, and one draw needn't show every extreme that they name: `adapter_ids`: adapter j belongs to owner j // 32. In every block b, at most 32 rows use adapters of one owner, and exactly 32 rows use adapters of one owner, the same owner for every block.
All inputs are finite; a program needn't handle non-finite values.
Results may differ from a plain program's by a relative error of at most 0.013.
Values may be sent and summed in bfloat16 or wider, within the bound.
A program may use at most 128 MiB of HBM per device.

v0:
```python
import jax
import jax.numpy as jnp
from jax import lax
from jax.sharding import PartitionSpec as P

ADAPTER_SCALING = 0.5


def per_device(attended, out_weight, adapter_ids, shrink_weight, expand_weight):
    inputs = attended[0]
    rows_all, features = inputs.shape
    owners = lax.axis_size("adapter")
    adapters_dev = shrink_weight.shape[0]
    capacity = rows_all // 2
    row_ids = adapter_ids[0]
    owning_adapter = row_ids // adapters_dev
    local_slot = row_ids % adapters_dev
    owner_hot = (owning_adapter[:, None] == jnp.arange(owners)[None, :]).astype(jnp.int32)
    running = jnp.cumsum(owner_hot, axis=0) - 1
    slot_of = owning_adapter * capacity + jnp.sum(running * owner_hot, axis=1)
    slot_ids = jnp.full((owners * capacity,), -1, jnp.int32).at[slot_of].set(local_slot)
    outgoing = jnp.zeros((owners * capacity, features), jnp.bfloat16).at[slot_of].set(inputs)
    recv_rows, recv_ids = (
        lax.all_to_all(outgoing, "adapter", split_axis=0, concat_axis=0, tiled=True),
        lax.all_to_all(slot_ids, "adapter", split_axis=0, concat_axis=0, tiled=True),
    )
    chosen = (recv_ids[:, None] == jnp.arange(adapters_dev)[None, :]).astype(jnp.float32)
    products = jnp.einsum(
        "nd,adr->nar", recv_rows, shrink_weight, preferred_element_type=jnp.float32
    )
    partial_sum = jnp.sum(products * chosen[:, :, None], axis=1)
    incoming_rows = lax.psum(partial_sum.astype(jnp.bfloat16), "tensor")
    spread = incoming_rows[:, None, :] * chosen.astype(jnp.bfloat16)[:, :, None]
    delta_rows = (
        ADAPTER_SCALING
        * jnp.einsum("nar,ard->nd", spread, expand_weight, preferred_element_type=jnp.float32)
    ).astype(jnp.bfloat16)
    returned = lax.all_to_all(delta_rows, "adapter", split_axis=0, concat_axis=0, tiled=True)
    home_delta = returned[slot_of]
    summed = lax.psum_scatter(
        jnp.dot(inputs, out_weight, preferred_element_type=jnp.float32).astype(jnp.bfloat16),
        "tensor",
        scatter_dimension=0,
        tiled=True,
    ).astype(jnp.float32)
    own_delta = lax.all_to_all(home_delta, "tensor", split_axis=0, concat_axis=1, tiled=True)
    projected = (summed + own_delta.astype(jnp.float32)).astype(jnp.bfloat16)
    return projected[None]


def solution(mesh):
    return jax.shard_map(
        per_device,
        mesh=mesh,
        in_specs=(
            P(("groups", "adapter"), None, "tensor"),
            P("tensor", None),
            P(("groups", "adapter"), None),
            P("adapter", "tensor", None),
            P("adapter", None, "tensor"),
        ),
        out_specs=P(("groups", "adapter"), "tensor", None),
        check_vma=False,
    )
```

profile of v0, /device:TPU:0, one launch (start us, length us, event | category | flops | bytes accessed | tf_op | source)
XLA Modules:
  0.0 101.6 jit_solution(7120884130361376732)
XLA Ops:
  6.5 0.7 and_select_fusion
  7.2 0.1 fusion.10
  7.3 0.1 reduce_window_sum.11
  7.4 0.2 select_reduce_fusion
  7.6 0.7 fusion.13
  8.3 0.8 scatter_custom_fusion.1
  9.1 0.7 all_to_all.35
  9.7 4.2 %all-to-all-start.1 = ((s32[4,32,1]{1,2,0:T(1,128)}), s32[4,32,1]{1,2,0:T(1,128)S(1)}, u32[]{:S(2)}, u32[]{:S(2)}) async-start(s32[4,32,1]{1,2,0:T(1,128)} %bitcast.10), calls=%async_computation.2 | async-start | bytes 4096 | tf_op jit(solution)/shard_map/all_to_all | solution.py:25
  13.9 1.8 %scatter_custom_fusion = bf16[128,2048]{1,0:T(8,128)(2,1)} fusion(s32[64]{0:T(128)S(1)} %fusion.13, bf16[1,64,2048]{2,1,0:T(8,128)(2,1)S(1)} %copy-done, bf16[]{:T(256)} %constant.36.clone.1), kind=kCustom, calls=%fused_computation.12 | custom fusion | bytes 786434 | tf_op jit(solution)/shard_map/scatter | solution.py:22
  15.8 1.8 %all-to-all-done.1 = s32[4,32,1]{1,2,0:T(1,128)S(1)} async-done(((s32[4,32,1]{1,2,0:T(1,128)}), s32[4,32,1]{1,2,0:T(1,128)S(1)}, u32[]{:S(2)}, u32[]{:S(2)}) %all-to-all-start.1) | async-done | bytes 544 | tf_op jit(solution)/shard_map/all_to_all | solution.py:25
  17.6 3.5 %all-to-all-start = ((bf16[4,32,2048]{2,1,0:T(8,128)(2,1)}), bf16[4,32,2048]{2,1,0:T(8,128)(2,1)S(1)}, u32[]{:S(2)}, u32[]{:S(2)}) async-start(bf16[4,32,2048]{2,1,0:T(8,128)(2,1)} %bitcast.5), calls=%async_computation.1 | async-start | bytes 1048576 | tf_op jit(solution)/shard_map/all_to_all | solution.py:24
  21.1 14.7 %convolution_convert_fusion = bf16[64,8192]{1,0:T(8,128)(2,1)} fusion(bf16[2048,8192]{1,0:T(8,128)(2,1)} %param.6, bf16[1,64,2048]{2,1,0:T(8,128)(2,1)S(1)} %copy-done), kind=kOutput, calls=%fused_computation.3 | convolution fusion | flops 2148007936 | bytes 34865152 | tf_op jit(solution)/shard_map/dot_general | solution.py:41
  35.8 0.5 broadcast.168
  36.3 0.7 reduce.3
  37.0 0.1 eq.40
  37.1 5.8 %fusion.16 = f32[128,2048]{0,1:S(1)} fusion(bf16[128,2048]{1,0:T(8,128)(2,1)S(1)} %bitcast.68, bf16[2048,2048]{0,1:T(8,128)(2,1)} %bitcast.65), kind=kOutput, calls=%fused_computation.41 | convolution fusion | flops 1073741824 | bytes 9961472
  42.9 0.2 multiply_reduce_fusion
  43.0 20.0 %psum.7 = bf16[128,64]{0,1:T(8,128)(2,1)S(1)} all-reduce(bf16[128,64]{0,1:T(8,128)(2,1)S(1)} %multiply_reduce_fusion), channel_id=1, replica_groups=mesh['groups'=2,'tensor'=4,'adapter'=4] {'tensor'}, use_global_device_ids=true, to_apply=%region_6.7 | all-reduce | flops 8192 | bytes 32768 | tf_op jit(solution)/shard_map/psum | solution.py:32
  63.0 5.5 %fusion.1 = bf16[128,2048]{1,0:T(8,128)(2,1)} fusion(bf16[32,64,2048]{2,1,0:T(8,128)(2,1)} %param.9, bf16[128,32]{0,1:T(8,128)(2,1)S(1)} %get-tuple-element.6, bf16[128,64]{0,1:T(8,128)(2,1)S(1)} %psum.7), kind=kOutput, calls=%fused_computation.6 | convolution fusion | flops 1074528256 | bytes 8937472 | tf_op jit(solution)/shard_map/nar,ard->nd/dot_general | solution.py:36
  68.6 3.6 %all-to-all-start.2 = ((bf16[4,32,2048]{2,1,0:T(8,128)(2,1)}), bf16[4,32,2048]{2,1,0:T(8,128)(2,1)S(1)}, u32[]{:S(2)}, u32[]{:S(2)}) async-start(bf16[4,32,2048]{2,1,0:T(8,128)(2,1)} %bitcast.12), calls=%async_computation.3 | async-start | bytes 1048576 | tf_op jit(solution)/shard_map/all_to_all | solution.py:38
  72.2 8.8 %all-to-all-done.2 = bf16[4,32,2048]{2,1,0:T(8,128)(2,1)S(1)} async-done(((bf16[4,32,2048]{2,1,0:T(8,128)(2,1)}), bf16[4,32,2048]{2,1,0:T(8,128)(2,1)S(1)}, u32[]{:S(2)}, u32[]{:S(2)}) %all-to-all-start.2) | async-done | bytes 524320 | tf_op jit(solution)/shard_map/all_to_all | solution.py:38
  81.0 0.7 gather_fusion
  81.8 11.2 %all_to_all.46 = bf16[4,16,2048]{2,1,0:T(8,128)(2,1)S(1)} all-to-all(bf16[4,16,2048]{2,1,0:T(8,128)(2,1)S(1)} %bitcast.70), channel_id=1, replica_groups=mesh['groups'=2,'tensor'=4,'adapter'=4] {'tensor'}, dimensions={0} | all-to-all | bytes 524288 | tf_op jit(solution)/shard_map/all_to_all | solution.py:46
  93.0 1.7 %fusion.3 = bf16[1,16,8192]{2,1,0:T(8,128)(2,1)} fusion(f32[16,8192]{1,0:T(8,128)S(1)} %bitcast.69, bf16[16,8192]{1,0:T(8,128)(2,1)} %reduce-scatter.2.cloned.1.call-done), kind=kLoop, calls=%fused_computation.11 | loop fusion | flops 393216 | bytes 1048576 | tf_op jit(solution)/shard_map/broadcast_in_dim | solution.py:48
  (10 shorter events, 0.2 us)
Async XLA Ops:
  6.5 7.4 %copy-start = (bf16[1,64,2048]{2,1,0:T(8,128)(2,1)S(1)}, bf16[1,64,2048]{2,1,0:T(8,128)(2,1)}, u32[]{:S(2)}) copy-start(bf16[1,64,2048]{2,1,0:T(8,128)(2,1)} %param.5) | copy-start | bytes 786436
  9.7 7.9 %all-to-all-start.1 = ((s32[4,32,1]{1,2,0:T(1,128)}), s32[4,32,1]{1,2,0:T(1,128)S(1)}, u32[]{:S(2)}, u32[]{:S(2)}) async-start(s32[4,32,1]{1,2,0:T(1,128)} %bitcast.10), calls=%async_computation.2 | async-start | bytes 4096 | tf_op jit(solution)/shard_map/all_to_all | solution.py:25
  17.6 19.5 %all-to-all-start = ((bf16[4,32,2048]{2,1,0:T(8,128)(2,1)}), bf16[4,32,2048]{2,1,0:T(8,128)(2,1)S(1)}, u32[]{:S(2)}, u32[]{:S(2)}) async-start(bf16[4,32,2048]{2,1,0:T(8,128)(2,1)} %bitcast.5), calls=%async_computation.1 | async-start | bytes 1048576 | tf_op jit(solution)/shard_map/all_to_all | solution.py:24
  21.1 72.0 %reduce-scatter.2.cloned.1.call-start = ((), (), s32[]{:S(2)}) async-start(), calls=%async_computation.5 | async-start | bytes 1310720 | tf_op jit(solution)/shard_map/reduce_scatter | solution.py:40
  68.6 12.4 %all-to-all-start.2 = ((bf16[4,32,2048]{2,1,0:T(8,128)(2,1)}), bf16[4,32,2048]{2,1,0:T(8,128)(2,1)S(1)}, u32[]{:S(2)}, u32[]{:S(2)}) async-start(bf16[4,32,2048]{2,1,0:T(8,128)(2,1)} %bitcast.12), calls=%async_computation.3 | async-start | bytes 1048576 | tf_op jit(solution)/shard_map/all_to_all | solution.py:38
Sparse Core Ops, SparseCore 0:
  35.9 29.7 reduce-scatter.1
where the time goes:
time: 102 us
  blocking collectives  31.2 us (31%)
  matrix products  26 us (25%)
  between operations  13.5 us (13%)
  starting transfers between devices  11.3 us (11%)
  waiting for transfers between devices  10.7 us (10%)
  local copies, waits for them, and re-layouts  4.64 us (5%)
  other arithmetic  4.3 us (4%)
    psum x1, blocking collectives, per_device(): incoming_rows = lax.psum(partial_sum.astype(jnp.bfloat16), 'tensor')  20 us
    dot_general x1, matrix products, per_device(): jnp.dot(inputs, out_weight, preferred_element_type=jnp.float32)  14.7 us
    all_to_all x1, blocking collectives, per_device(): lax.all_to_all(home_delta, 'tensor', split_axis=0, concat_axis=1, tiled=T...  11.2 us
    all_to_all x1, waiting for transfers between devices, per_device(): lax.all_to_all(delta_rows, 'adapter', split_axis=0, concat_axis=0, tiled=...  8.84 us
    unnamed x1, matrix products  5.77 us
    dot_general x1, matrix products, per_device(): jnp.einsum('nar,ard->nd', spread, expand_weight, preferred_element_type=j...  5.54 us
    all_to_all x1, starting transfers between devices, per_device(): lax.all_to_all(slot_ids, 'adapter', split_axis=0, concat_axis=0, tiled=True)  4.21 us
    all_to_all x1, starting transfers between devices, per_device(): lax.all_to_all(delta_rows, 'adapter', split_axis=0, concat_axis=0, tiled=...  3.59 us
  transfers between devices with their start and end apart: 4, of which 2 were waited for; matrix products, arithmetic and copies ran while one was open for 30% of the time, Pallas kernels for 0%

commit v1 on v0

--- a/solution.py
+++ b/solution.py
@@ -1,12 +1,340 @@
+import functools
+
 import jax
 import jax.numpy as jnp
 from jax import lax
+from jax.experimental import pallas as pl
+from jax.experimental.pallas import tpu as pltpu
 from jax.sharding import PartitionSpec as P
 
 ADAPTER_SCALING = 0.5
-
-
-def per_device(attended, out_weight, adapter_ids, shrink_weight, expand_weight):
+MESH = pl.DeviceIdType.MESH
+TILE = 256
+VMEM_LIMIT = 60 * 2**20
+F32 = jnp.float32
+BF16 = jnp.bfloat16
+
+
+def fused_kernel(
+    owners, tensors, base_chunks, expand_chunks,
+    ids_ref, att_hbm, w_hbm, s_hbm, e_hbm, out_ref,
+    att, w, s, e, slots, slot_ids, got, got_ids, home_hot,
+    part, part_in, low, low_in, spread, corr, ret, home, home_in,
+    att_sem, w_sem, s_sem, e_sem,
+    rows_send, rows_recv, ids_send, ids_recv, low_send, low_recv,
+    part_send, part_recv, corr_send, corr_recv, home_send, home_recv,
+):
+    rows, features = att.shape
+    width = w.shape[1]
+    low_width, slice_width = e.shape
+    lanes = slot_ids.shape[1]
+    capacity = rows // 2
+    n_slots = owners * capacity
+    rows_dev = rows // tensors
+    rank = lanes // 2
+    adapters = low_width // rank
+    chunk = width // base_chunks
+    piece = slice_width // expand_chunks
+    halves = s_sem.shape[0]
+    half = low_width // halves
+    me = lax.axis_index("adapter")
+    plane = lax.axis_index("tensor")
+
+    def load_w(c):
+        cols = pl.ds(c * chunk, chunk)
+        return pltpu.make_async_copy(w_hbm.at[:, cols], w.at[:, cols], w_sem.at[c])
+
+    def load_s(h):
+        some = pl.ds(h * half, half)
+        return pltpu.make_async_copy(s_hbm.at[some], s.at[some], s_sem.at[h])
+
+    def load_e(c):
+        cols = pl.ds(c * piece, piece)
+        return pltpu.make_async_copy(e_hbm.at[:, cols], e.at[:, cols], e_sem.at[c])
+
+    load_att = pltpu.make_async_copy(att_hbm, att, att_sem)
+    load_att.start()
+    load_w(0).start()
+    for h in range(halves):
+        load_s(h).start()
+    load_w(1).start()
+
+    barrier = pltpu.get_barrier_semaphore()
+    for j in range(1, owners):
+        pl.semaphore_signal(barrier, inc=1, device_id={"adapter": lax.rem(me + j, owners)}, device_id_type=MESH)
+    for j in range(1, tensors):
+        pl.semaphore_signal(barrier, inc=1, device_id={"tensor": lax.rem(plane + j, tensors)}, device_id_type=MESH)
+
+    ids = ids_ref[...]
+    relative = lax.rem(lax.div(ids, adapters) - me + owners, owners)
+    below = lax.broadcasted_iota(jnp.int32, (rows, rows), 0)
+    along = lax.broadcasted_iota(jnp.int32, (rows, rows), 1)
+
+    def as_column(row):
+        return jnp.sum(jnp.where(below == along, row, 0), axis=1, keepdims=True)
+
+    same = as_column(relative) == relative
+    running = jnp.sum(jnp.where(same & (below < along), 1, 0), axis=0, keepdims=True)
+    slot_of = relative * capacity + running
+    hot = lax.broadcasted_iota(jnp.int32, (n_slots, rows), 0) == slot_of
+    home_hot[...] = jnp.where(
+        lax.broadcasted_iota(jnp.int32, (rows, n_slots), 1) == as_column(slot_of), 1.0, 0.0
+    ).astype(BF16)
+    local_slot = jnp.sum(jnp.where(hot, lax.rem(ids, adapters) + 1, 0), axis=1, keepdims=True) - 1
+    slot_ids[...] = jnp.broadcast_to(local_slot, (n_slots, lanes))
+    load_att.wait()
+    hot = jnp.where(hot, 1.0, 0.0).astype(BF16)
+
+    @pl.loop(0, features // TILE)
+    def _(i):
+        cols = pl.ds(pl.multiple_of(i * TILE, TILE), TILE)
+        slots[:, cols] = jnp.dot(hot, att[:, cols], preferred_element_type=F32).astype(BF16)
+
+    pl.semaphore_wait(barrier, owners - 1 + tensors - 1)
+
+    def send_rows(j):
+        mine = pl.ds(j * capacity, capacity)
+        to = {"adapter": lax.rem(me + j, owners)}
+        return (
+            pltpu.make_async_remote_copy(
+                src_ref=slots.at[mine], dst_ref=got.at[mine],
+                send_sem=rows_send.at[j - 1], recv_sem=rows_recv.at[j - 1],
+                device_id=to, device_id_type=MESH,
+            ),
+            pltpu.make_async_remote_copy(
+                src_ref=slot_ids.at[mine], dst_ref=got_ids.at[mine],
+                send_sem=ids_send.at[j - 1], recv_sem=ids_recv.at[j - 1],
+                device_id=to, device_id_type=MESH,
+            ),
+        )
+
+    def send_part(j, c):
+        cols = pl.ds(c * chunk, chunk)
+        to = lax.rem(plane + j, tensors)
+        return pltpu.make_async_remote_copy(
+            src_ref=part.at[to, :, cols], dst_ref=part_in.at[j - 1, :, cols],
+            send_sem=part_send.at[j - 1, c], recv_sem=part_recv.at[j - 1, c],
+            device_id={"tensor": to}, device_id_type=MESH,
+        )
+
+    def send_low(j):
+        return pltpu.make_async_remote_copy(
+            src_ref=low, dst_ref=low_in.at[j - 1],
+            send_sem=low_send.at[j - 1], recv_sem=low_recv.at[j - 1],
+            device_id={"tensor": lax.rem(plane + j, tensors)}, device_id_type=MESH,
+        )
+
+    def send_corr(j, c):
+        mine, cols = pl.ds(j * capacity, capacity), pl.ds(c * piece, piece)
+        return pltpu.make_async_remote_copy(
+            src_ref=corr.at[mine, cols], dst_ref=ret.at[mine, cols],
+            send_sem=corr_send.at[j - 1, c], recv_sem=corr_recv.at[j - 1, c],
+            device_id={"adapter": lax.rem(me - j + owners, owners)}, device_id_type=MESH,
+        )
+
+    def send_home(j, c):
+        cols = pl.ds(c * piece, piece)
+        to = lax.rem(plane + j, tensors)
+        return pltpu.make_async_remote_copy(
+            src_ref=home.at[to, :, cols], dst_ref=home_in.at[j - 1, :, cols],
+            send_sem=home_send.at[j - 1, c], recv_sem=home_recv.at[j - 1, c],
+            device_id={"tensor": to}, device_id_type=MESH,
+        )
+
+    for j in range(1, owners):
+        for copy in send_rows(j):
+            copy.start()
+    got[pl.ds(0, capacity)] = slots[pl.ds(0, capacity)]
+    got_ids[pl.ds(0, capacity)] = slot_ids[pl.ds(0, capacity)]
+
+    def base(c):
+        if c + 2 < base_chunks:
+            load_w(c + 2).start()
+        load_w(c).wait()
+
+        @pl.loop(0, chunk // TILE)
+        def _(i):
+            cols = pl.ds(pl.multiple_of(c * chunk + i * TILE, TILE), TILE)
+            product = jnp.dot(att[...], w[:, cols], preferred_element_type=F32).astype(BF16)
+            for to in range(tensors):
+                part[to, :, cols] = product[to * rows_dev:(to + 1) * rows_dev]
+
+        for j in range(1, tensors):
+            send_part(j, c).start()
+
+    def shrink():
+        for j in range(1, owners):
+            for copy in send_rows(j):
+                copy.wait_recv()
+        for h in range(halves):
+            load_s(h).wait()
+        lane_parity = lax.div(lax.broadcasted_iota(jnp.int32, (n_slots, lanes), 1), rank)
+        wanted = got_ids[...] - lane_parity
+
+        def step(i, total):
+            some = pl.ds(pl.multiple_of(i * TILE, TILE), TILE)
+            products = lax.dot_general(
+                got[...], s[some, :], (((1,), (1,)), ((), ())), preferred_element_type=F32
+            )
+            for k in range(TILE // lanes):
+                here = products[:, k * lanes:(k + 1) * lanes]
+                total += jnp.where(wanted == 2 * (i * (TILE // lanes) + k), here, 0.0)
+            return total
+
+        total = lax.fori_loop(0, low_width // TILE, step, jnp.zeros((n_slots, lanes), F32))
+        low[...] = total.astype(BF16)
+        for j in range(1, tensors):
+            send_low(j).start()
+
+    def expand():
+        shrunk = low[...].astype(F32)
+        for j in range(1, tensors):
+            send_low(j).wait_recv()
+            shrunk += low_in[j - 1].astype(F32)
+        pair = lax.shift_right_arithmetic(got_ids[...], 1)
+        for p in range(low_width // lanes):
+            spread[:, p * lanes:(p + 1) * lanes] = jnp.where(pair == p, shrunk, 0.0).astype(BF16)
+        for c in range(expand_chunks):
+            load_e(c).wait()
+
+            @pl.loop(0, piece // TILE)
+            def _(i):
+                cols = pl.ds(pl.multiple_of(c * piece + i * TILE, TILE), TILE)
+                corr[:, cols] = (
+                    ADAPTER_SCALING * jnp.dot(spread[...], e[:, cols], preferred_element_type=F32)
+                ).astype(BF16)
+
+            for j in range(1, owners):
+                send_corr(j, c).start()
+        ret[pl.ds(0, capacity)] = corr[pl.ds(0, capacity)]
+
+    def merge(c):
+        for j in range(1, owners):
+            send_corr(j, c).wait_recv()
+        cols = pl.ds(c * piece, piece)
+        merged = jnp.dot(home_hot[...], ret[:, cols], preferred_element_type=F32).astype(BF16)
+        for to in range(tensors):
+            home[to, :, cols] = merged[to * rows_dev:(to + 1) * rows_dev]
+        for j in range(1, tensors):
+            send_home(j, c).start()
+
+    base(0)
+    base(1)
+    for c in range(expand_chunks):
+        load_e(c).start()
+    base(2)
+    shrink()
+    base(3)
+    base(4)
+    expand()
+    for c in range(5, base_chunks):
+        base(c)
+    for c in range(expand_chunks):
+        merge(c)
+
+    for c in range(base_chunks):
+        cols = pl.ds(c * chunk, chunk)
+        total = part[plane, :, cols].astype(F32)
+        for j in range(1, tensors):
+            send_part(j, c).wait_recv()
+            total += part_in[j - 1, :, cols].astype(F32)
+        out_ref[:, cols] = total
+    for j in range(tensors):
+        for c in range(expand_chunks):
+            if j:
+                send_home(j, c).wait_recv()
+        source = lax.rem(plane - j + tensors, tensors)
+        cols = pl.ds(pl.multiple_of(source * slice_width, slice_width), slice_width)
+        own = home_in[j - 1] if j else home[plane]
+        out_ref[:, cols] += own.astype(F32)
+
+    for j in range(1, owners):
+        for copy in send_rows(j):
+            copy.wait_send()
+        for c in range(expand_chunks):
+            send_corr(j, c).wait_send()
+    for j in range(1, tensors):
+        send_low(j).wait_send()
+        for c in range(base_chunks):
+            send_part(j, c).wait_send()
+        for c in range(expand_chunks):
+            send_home(j, c).wait_send()
+
+
+def fused(attended, out_weight, adapter_ids, shrink_weight, expand_weight):
+    owners, tensors = lax.axis_size("adapter"), lax.axis_size("tensor")
+    rows, features = attended.shape[1:]
+    width = out_weight.shape[1]
+    adapters, rank, slice_width = expand_weight.shape
+    low_width, lanes = adapters * rank, 2 * rank
+    n_slots, rows_dev = owners * (rows // 2), rows // tensors
+    base_chunks, expand_chunks, halves = 8, 4, 2
+    dma = lambda *shape: pltpu.SemaphoreType.DMA(shape)
+    pairs = lambda n: [dma(n), dma(n)]
+    grids = lambda n, m: [dma(n, m), dma(n, m)]
+    vmem = lambda *shape: pltpu.VMEM(shape, BF16)
+    ints = lambda *shape: pltpu.VMEM(shape, jnp.int32)
+    summed = pl.pallas_call(
+        functools.partial(fused_kernel, owners, tensors, base_chunks, expand_chunks),
+        out_shape=jax.ShapeDtypeStruct((rows_dev, width), F32),
+        in_specs=[pl.BlockSpec(memory_space=pltpu.VMEM)] + [pl.BlockSpec(memory_space=pl.ANY)] * 4,
+        out_specs=pl.BlockSpec(memory_space=pltpu.VMEM),
+        scratch_shapes=[
+            vmem(rows, features),
+            vmem(features, width),
+            vmem(low_width, features),
+            vmem(low_width, slice_width),
+            vmem(n_slots, features),
+            ints(n_slots, lanes),
+            vmem(n_slots, features),
+            ints(n_slots, lanes),
+            vmem(rows, n_slots),
+            vmem(tensors, rows_dev, width),
+            vmem(tensors - 1, rows_dev, width),
+            vmem(n_slots, lanes),
+            vmem(tensors - 1, n_slots, lanes),
+            vmem(n_slots, low_width),
+            vmem(n_slots, slice_width),
+            vmem(n_slots, slice_width),
+            vmem(tensors, rows_dev, slice_width),
+            vmem(tensors - 1, rows_dev, slice_width),
+            pltpu.SemaphoreType.DMA,
+            dma(base_chunks),
+            dma(halves),
+            dma(expand_chunks),
+            *pairs(owners - 1),
+            *pairs(owners - 1),
+            *pairs(tensors - 1),
+            *grids(tensors - 1, base_chunks),
+            *grids(owners - 1, expand_chunks),
+            *grids(tensors - 1, expand_chunks),
+        ],
+        compiler_params=pltpu.CompilerParams(
+            collective_id=0, has_side_effects=True, vmem_limit_bytes=VMEM_LIMIT
+        ),
+    )(
+        adapter_ids,
+        attended[0],
+        out_weight,
+        jnp.swapaxes(shrink_weight, 1, 2).reshape(low_width, features),
+        expand_weight.reshape(low_width, slice_width),
+    )
+    return summed.astype(BF16)[None]
+
+
+def fits(attended, out_weight, shrink_weight, expand_weight):
+    owners, tensors = lax.axis_size("adapter"), lax.axis_size("tensor")
+    rows, features = attended.shape[1:]
+    width, slice_width = out_weight.shape[1], expand_weight.shape[2]
+    low_width = expand_weight.shape[0] * expand_weight.shape[1]
+    slots = owners * (rows // 2)
+    values = out_weight.size + shrink_weight.size + expand_weight.size
+    values += rows * (features + 4 * width) + slots * (2 * features + low_width + 3 * slice_width)
+    tiled = rows % (16 * tensors) == 0 and width % (8 * TILE) == 0 and slice_width % (4 * TILE) == 0
+    return tiled and features % TILE == 0 and 2 * values <= VMEM_LIMIT
+
+
+def plain(attended, out_weight, adapter_ids, shrink_weight, expand_weight):
     inputs = attended[0]
     rows_all, features = inputs.shape
     owners = lax.axis_size("adapter")
@@ -48,6 +376,11 @@
     return projected[None]
 
 
+def per_device(attended, out_weight, adapter_ids, shrink_weight, expand_weight):
+    form = fused if fits(attended, out_weight, shrink_weight, expand_weight) else plain
+    return form(attended, out_weight, adapter_ids, shrink_weight, expand_weight)
+
+
 def solution(mesh):
     return jax.shard_map(
         per_device,

time: 102 us -> 46.8 us (0.46)
  Pallas kernels: 0 us -> 44.8 us
  blocking collectives: 31.2 us -> 0 us
  matrix products: 26 us -> 0 us
  between operations: 13.5 us -> 0.01 us
  starting transfers between devices: 11.3 us -> 0 us
  waiting for transfers between devices: 10.7 us -> 0 us
  local copies, waits for them, and re-layouts: 4.64 us -> 0 us
  other arithmetic: 4.3 us -> 1.77 us
    pallas_call x0 -> x1, Pallas kernels: none -> 44.8 us  [fused(): pl.pallas_call(functools.partial(fused_kernel, owners, tensors, base_chun...]
    dot_general x2 -> x0, matrix products: 20.2 us -> none  [the longest x1 14.7 us: per_device(): jnp.dot(inputs, out_weight, preferred_element_type=jnp.float32)]
    psum x1 -> x0, blocking collectives: 20 us -> none  [per_device(): incoming_rows = lax.psum(partial_sum.astype(jnp.bfloat16), 'tensor')]
    all_to_all x3 -> x0, starting transfers between devices: 11.3 us -> none  [the longest x1 4.21 us: per_device(): lax.all_to_all(slot_ids, 'adapter', split_axis=0, concat_axis=0, tiled=True)]
    all_to_all x1 -> x0, blocking collectives: 11.2 us -> none  [per_device(): lax.all_to_all(home_delta, 'tensor', split_axis=0, concat_axis=1, tiled=T...]
    all_to_all x3 -> x0, waiting for transfers between devices: 10.7 us -> none  [the longest x1 8.84 us: per_device(): lax.all_to_all(delta_rows, 'adapter', split_axis=0, concat_axis=0, tiled=...]
    unnamed x1 -> x0, matrix products: 5.77 us -> none
    scatter x2 -> x0, local copies, waits for them, and re-layouts: 2.6 us -> none  [the longest x1 1.83 us: per_device(): jnp.zeros((owners * capacity, features), jnp.bfloat16).at[slot_of]]
  transfers between devices with their start and end apart: 4 -> 0, of which waited for: 2 -> 0; matrix products, arithmetic and copies ran while one was open for 30% -> 0% of each run, Pallas kernels for 0% -> 0%
where the time goes in v1:
time: 46.8 us; the launch traced here: 46.6 us
  Pallas kernels  44.8 us (96%)
  other arithmetic  1.77 us (4%)
    pallas_call x1, Pallas kernels, fused(): pl.pallas_call(functools.partial(fused_kernel, owners, tensors, base_chun...  44.8 us
    broadcast_in_dim x1, other arithmetic, fused(): return summed.astype(BF16)[None]  1.77 us

profile of v1, /device:TPU:0, one launch (start us, length us, event | category | flops | bytes accessed | tf_op | source)
XLA Modules:
  0.0 46.6 jit_solution(17728558717187187270)
XLA Ops:
  0.0 44.8 %shard_map.55 = f32[16,8192]{1,0:T(8,128)} custom-call(s32[1,64]{1,0:T(1,128)} %ids_ref.1, bf16[64,2048]{1,0:T(8,128)(2,1)} %bitcast.9, bf16[2048,8192]{1,0:T(8,128)(2,1)} %w_hbm.1, bf16[2048,2048]{1,0:T(8,128)(2,1)} %bitcast.7, bf16[2048,2048]{1,0:T(8,128)(2,1)} %bitcast.8), custom_call_target="tpu_custom_call" | custom-call | tf_op jit(solution)/shard_map/pallas_call | solution.py:277
  44.8 1.8 %convert_bitcast_fusion = bf16[1,16,8192]{2,1,0:T(8,128)(2,1)} fusion(f32[16,8192]{1,0:T(8,128)} %shard_map.55), kind=kLoop, calls=%fused_computation | loop fusion | flops 131072 | bytes 786432 | tf_op jit(solution)/shard_map/broadcast_in_dim | solution.py:322

commit v2 on v1

--- a/solution.py
+++ b/solution.py
@@ -10,19 +10,22 @@
 ADAPTER_SCALING = 0.5
 MESH = pl.DeviceIdType.MESH
 TILE = 256
+BASE_TILE = 512
+WIDE = 2048
+EARLY = 0
 VMEM_LIMIT = 60 * 2**20
 F32 = jnp.float32
 BF16 = jnp.bfloat16
 
 
 def fused_kernel(
-    owners, tensors, base_chunks, expand_chunks,
+    owners, tensors, base_chunks, expand_chunks, row_chunks,
     ids_ref, att_hbm, w_hbm, s_hbm, e_hbm, out_ref,
     att, w, s, e, slots, slot_ids, got, got_ids, home_hot,
-    part, part_in, low, low_in, spread, corr, ret, home, home_in,
+    part, pair_in, cross, cross_in, low, low_in, spread, corr, ret, home, home_in,
     att_sem, w_sem, s_sem, e_sem,
     rows_send, rows_recv, ids_send, ids_recv, low_send, low_recv,
-    part_send, part_recv, corr_send, corr_recv, home_send, home_recv,
+    pair_send, pair_recv, cross_send, cross_recv, corr_send, corr_recv, home_send, home_recv,
 ):
     rows, features = att.shape
     width = w.shape[1]
@@ -35,18 +38,20 @@
     adapters = low_width // rank
     chunk = width // base_chunks
     piece = slice_width // expand_chunks
-    halves = s_sem.shape[0]
-    half = low_width // halves
+    strip = features // row_chunks
     me = lax.axis_index("adapter")
     plane = lax.axis_index("tensor")
+    partner = plane + 1 - 2 * lax.rem(plane, 2)
+    across = lax.rem(plane + 2, tensors)
+    partner_across = lax.rem(partner + 2, tensors)
 
     def load_w(c):
         cols = pl.ds(c * chunk, chunk)
         return pltpu.make_async_copy(w_hbm.at[:, cols], w.at[:, cols], w_sem.at[c])
 
-    def load_s(h):
-        some = pl.ds(h * half, half)
-        return pltpu.make_async_copy(s_hbm.at[some], s.at[some], s_sem.at[h])
+    def load_s(k):
+        cols = pl.ds(k * strip, strip)
+        return pltpu.make_async_copy(s_hbm.at[:, cols], s.at[:, cols], s_sem.at[k])
 
     def load_e(c):
         cols = pl.ds(c * piece, piece)
@@ -54,10 +59,12 @@
 
     load_att = pltpu.make_async_copy(att_hbm, att, att_sem)
     load_att.start()
-    load_w(0).start()
-    for h in range(halves):
-        load_s(h).start()
-    load_w(1).start()
+    for c in range(EARLY):
+        load_w(c).start()
+    for k in range(row_chunks):
+        load_s(k).start()
+    for c in range(EARLY, EARLY + 2):
+        load_w(c).start()
 
     barrier = pltpu.get_barrier_semaphore()
     for j in range(1, owners):
@@ -90,31 +97,51 @@
         cols = pl.ds(pl.multiple_of(i * TILE, TILE), TILE)
         slots[:, cols] = jnp.dot(hot, att[:, cols], preferred_element_type=F32).astype(BF16)
 
+    def compute_base(c):
+        load_w(c).wait()
+
+        @pl.loop(0, chunk // BASE_TILE)
+        def _(i):
+            cols = pl.ds(pl.multiple_of(c * chunk + i * BASE_TILE, BASE_TILE), BASE_TILE)
+            product = jnp.dot(att[...], w[:, cols], preferred_element_type=F32).astype(BF16)
+            for to in range(tensors):
+                part[to, :, cols] = product[to * rows_dev:(to + 1) * rows_dev]
+
+    for c in range(EARLY):
+        compute_base(c)
+
     pl.semaphore_wait(barrier, owners - 1 + tensors - 1)
 
-    def send_rows(j):
+    def send_rows(j, k):
+        mine, cols = pl.ds(j * capacity, capacity), pl.ds(k * strip, strip)
+        return pltpu.make_async_remote_copy(
+            src_ref=slots.at[mine, cols], dst_ref=got.at[mine, cols],
+            send_sem=rows_send.at[j - 1, k], recv_sem=rows_recv.at[j - 1, k],
+            device_id={"adapter": lax.rem(me + j, owners)}, device_id_type=MESH,
+        )
+
+    def send_ids(j):
         mine = pl.ds(j * capacity, capacity)
-        to = {"adapter": lax.rem(me + j, owners)}
-        return (
-            pltpu.make_async_remote_copy(
-                src_ref=slots.at[mine], dst_ref=got.at[mine],
-                send_sem=rows_send.at[j - 1], recv_sem=rows_recv.at[j - 1],
-                device_id=to, device_id_type=MESH,
-            ),
-            pltpu.make_async_remote_copy(
-                src_ref=slot_ids.at[mine], dst_ref=got_ids.at[mine],
-                send_sem=ids_send.at[j - 1], recv_sem=ids_recv.at[j - 1],
-                device_id=to, device_id_type=MESH,
-            ),
-        )
-
-    def send_part(j, c):
+        return pltpu.make_async_remote_copy(
+            src_ref=slot_ids.at[mine], dst_ref=got_ids.at[mine],
+            send_sem=ids_send.at[j - 1], recv_sem=ids_recv.at[j - 1],
+            device_id={"adapter": lax.rem(me + j, owners)}, device_id_type=MESH,
+        )
+
+    def send_pair(i, c):
         cols = pl.ds(c * chunk, chunk)
-        to = lax.rem(plane + j, tensors)
-        return pltpu.make_async_remote_copy(
-            src_ref=part.at[to, :, cols], dst_ref=part_in.at[j - 1, :, cols],
-            send_sem=part_send.at[j - 1, c], recv_sem=part_recv.at[j - 1, c],
-            device_id={"tensor": to}, device_id_type=MESH,
+        return pltpu.make_async_remote_copy(
+            src_ref=part.at[partner_across if i else partner, :, cols], dst_ref=pair_in.at[i, :, cols],
+            send_sem=pair_send.at[i, c], recv_sem=pair_recv.at[i, c],
+            device_id={"tensor": partner}, device_id_type=MESH,
+        )
+
+    def send_cross(c):
+        cols = pl.ds(c * chunk, chunk)
+        return pltpu.make_async_remote_copy(
+            src_ref=cross.at[:, cols], dst_ref=cross_in.at[:, cols],
+            send_sem=cross_send.at[c], recv_sem=cross_recv.at[c],
+            device_id={"tensor": across}, device_id_type=MESH,
         )
 
     def send_low(j):
@@ -141,65 +168,67 @@
             device_id={"tensor": to}, device_id_type=MESH,
         )
 
-    for j in range(1, owners):
-        for copy in send_rows(j):
-            copy.start()
-    got[pl.ds(0, capacity)] = slots[pl.ds(0, capacity)]
-    got_ids[pl.ds(0, capacity)] = slot_ids[pl.ds(0, capacity)]
+    def send_base(c):
+        send_pair(1, c).start()
+        send_pair(0, c).start()
 
     def base(c):
         if c + 2 < base_chunks:
             load_w(c + 2).start()
-        load_w(c).wait()
-
-        @pl.loop(0, chunk // TILE)
-        def _(i):
-            cols = pl.ds(pl.multiple_of(c * chunk + i * TILE, TILE), TILE)
-            product = jnp.dot(att[...], w[:, cols], preferred_element_type=F32).astype(BF16)
-            for to in range(tensors):
-                part[to, :, cols] = product[to * rows_dev:(to + 1) * rows_dev]
-
-        for j in range(1, tensors):
-            send_part(j, c).start()
-
-    def shrink():
+        compute_base(c)
+        send_base(c)
+
+    def forward(c):
+        send_pair(1, c).wait_recv()
+        cols = pl.ds(c * chunk, chunk)
+        cross[:, cols] = (part[across, :, cols].astype(F32) + pair_in[1, :, cols].astype(F32)).astype(BF16)
+        send_cross(c).start()
+
+    lane_parity = lax.div(lax.broadcasted_iota(jnp.int32, (n_slots, lanes), 1), rank)
+
+    def shrink(k, total):
+        load_s(k).wait()
         for j in range(1, owners):
-            for copy in send_rows(j):
-                copy.wait_recv()
-        for h in range(halves):
-            load_s(h).wait()
-        lane_parity = lax.div(lax.broadcasted_iota(jnp.int32, (n_slots, lanes), 1), rank)
+            send_rows(j, k).wait_recv()
         wanted = got_ids[...] - lane_parity
 
         def step(i, total):
-            some = pl.ds(pl.multiple_of(i * TILE, TILE), TILE)
+            some = pl.ds(pl.multiple_of(i * WIDE, WIDE), WIDE)
             products = lax.dot_general(
-                got[...], s[some, :], (((1,), (1,)), ((), ())), preferred_element_type=F32
+                got[:, k * strip:(k + 1) * strip], s[some, k * strip:(k + 1) * strip],
+                (((1,), (1,)), ((), ())), preferred_element_type=F32,
             )
-            for k in range(TILE // lanes):
-                here = products[:, k * lanes:(k + 1) * lanes]
-                total += jnp.where(wanted == 2 * (i * (TILE // lanes) + k), here, 0.0)
+            for p in range(WIDE // lanes):
+                here = products[:, p * lanes:(p + 1) * lanes]
+                total += jnp.where(wanted == 2 * (i * (WIDE // lanes) + p), here, 0.0)
             return total
 
-        total = lax.fori_loop(0, low_width // TILE, step, jnp.zeros((n_slots, lanes), F32))
-        low[...] = total.astype(BF16)
+        return lax.fori_loop(0, low_width // WIDE, step, total)
+
+    def send_total(total):
+        both = total + pltpu.roll(total, rank, 1)
+        packed = jnp.where(lane_parity[:n_slots // 2] == 0, both[:n_slots // 2], both[n_slots // 2:])
+        low[...] = packed.astype(BF16)
         for j in range(1, tensors):
             send_low(j).start()
 
     def expand():
-        shrunk = low[...].astype(F32)
+        packed = low[...].astype(F32)
         for j in range(1, tensors):
             send_low(j).wait_recv()
-            shrunk += low_in[j - 1].astype(F32)
-        pair = lax.shift_right_arithmetic(got_ids[...], 1)
+            packed += low_in[j - 1].astype(F32)
+        turned = pltpu.roll(packed, rank, 1)
+        first = lane_parity[:n_slots // 2] == 0
+        shrunk = jnp.concatenate([jnp.where(first, packed, turned), jnp.where(first, turned, packed)], axis=0)
+        wanted = got_ids[...] - lane_parity
         for p in range(low_width // lanes):
-            spread[:, p * lanes:(p + 1) * lanes] = jnp.where(pair == p, shrunk, 0.0).astype(BF16)
+            spread[:, p * lanes:(p + 1) * lanes] = jnp.where(wanted == 2 * p, shrunk, 0.0).astype(BF16)
         for c in range(expand_chunks):
             load_e(c).wait()
 
-            @pl.loop(0, piece // TILE)
+            @pl.loop(0, 1)
             def _(i):
-                cols = pl.ds(pl.multiple_of(c * piece + i * TILE, TILE), TILE)
+                cols = pl.ds(c * piece, piece)
                 corr[:, cols] = (
                     ADAPTER_SCALING * jnp.dot(spread[...], e[:, cols], preferred_element_type=F32)
                 ).astype(BF16)
@@ -218,27 +247,49 @@
         for j in range(1, tensors):
             send_home(j, c).start()
 
+    for j in range(1, owners):
+        send_ids(j).start()
+    for k in range(row_chunks):
+        for j in range(1, owners):
+            send_rows(j, k).start()
+    got[pl.ds(0, capacity)] = slots[pl.ds(0, capacity)]
+    got_ids[pl.ds(0, capacity)] = slot_ids[pl.ds(0, capacity)]
+    for c in range(expand_chunks):
+        load_e(c).start()
     base(0)
     base(1)
-    for c in range(expand_chunks):
-        load_e(c).start()
     base(2)
-    shrink()
     base(3)
+    forward(0)
+    for j in range(1, owners):
+        send_ids(j).wait_recv()
+    total = jnp.zeros((n_slots, lanes), F32)
+    for k in range(row_chunks):
+        total = shrink(k, total)
+    send_total(total)
+    forward(1)
     base(4)
+    base(5)
+    base(6)
+    forward(2)
     expand()
-    for c in range(5, base_chunks):
-        base(c)
-    for c in range(expand_chunks):
-        merge(c)
+    base(7)
+    forward(3)
+    forward(4)
+    forward(5)
+    merge(0)
+    forward(6)
+    merge(1)
+    forward(7)
+    merge(2)
+    merge(3)
 
     for c in range(base_chunks):
         cols = pl.ds(c * chunk, chunk)
-        total = part[plane, :, cols].astype(F32)
-        for j in range(1, tensors):
-            send_part(j, c).wait_recv()
-            total += part_in[j - 1, :, cols].astype(F32)
-        out_ref[:, cols] = total
+        send_pair(0, c).wait_recv()
+        send_cross(c).wait_recv()
+        total = part[plane, :, cols].astype(F32) + pair_in[0, :, cols].astype(F32)
+        out_ref[:, cols] = total + cross_in[:, cols].astype(F32)
     for j in range(tensors):
         for c in range(expand_chunks):
             if j:
@@ -249,16 +300,19 @@
         out_ref[:, cols] += own.astype(F32)
 
     for j in range(1, owners):
-        for copy in send_rows(j):
-            copy.wait_send()
+        send_ids(j).wait_send()
+        for k in range(row_chunks):
+            send_rows(j, k).wait_send()
         for c in range(expand_chunks):
             send_corr(j, c).wait_send()
     for j in range(1, tensors):
         send_low(j).wait_send()
-        for c in range(base_chunks):
-            send_part(j, c).wait_send()
         for c in range(expand_chunks):
             send_home(j, c).wait_send()
+    for c in range(base_chunks):
+        send_pair(0, c).wait_send()
+        send_pair(1, c).wait_send()
+        send_cross(c).wait_send()
 
 
 def fused(attended, out_weight, adapter_ids, shrink_weight, expand_weight):
@@ -268,14 +322,14 @@
     adapters, rank, slice_width = expand_weight.shape
     low_width, lanes = adapters * rank, 2 * rank
     n_slots, rows_dev = owners * (rows // 2), rows // tensors
-    base_chunks, expand_chunks, halves = 8, 4, 2
+    base_chunks, expand_chunks, row_chunks = 8, 4, 1
     dma = lambda *shape: pltpu.SemaphoreType.DMA(shape)
     pairs = lambda n: [dma(n), dma(n)]
     grids = lambda n, m: [dma(n, m), dma(n, m)]
     vmem = lambda *shape: pltpu.VMEM(shape, BF16)
     ints = lambda *shape: pltpu.VMEM(shape, jnp.int32)
     summed = pl.pallas_call(
-        functools.partial(fused_kernel, owners, tensors, base_chunks, expand_chunks),
+        functools.partial(fused_kernel, owners, tensors, base_chunks, expand_chunks, row_chunks),
         out_shape=jax.ShapeDtypeStruct((rows_dev, width), F32),
         in_specs=[pl.BlockSpec(memory_space=pltpu.VMEM)] + [pl.BlockSpec(memory_space=pl.ANY)] * 4,
         out_specs=pl.BlockSpec(memory_space=pltpu.VMEM),
@@ -290,9 +344,11 @@
             ints(n_slots, lanes),
             vmem(rows, n_slots),
             vmem(tensors, rows_dev, width),
-            vmem(tensors - 1, rows_dev, width),
-            vmem(n_slots, lanes),
-            vmem(tensors - 1, n_slots, lanes),
+            vmem(2, rows_dev, width),
+            vmem(rows_dev, width),
+            vmem(rows_dev, width),
+            vmem(n_slots // 2, lanes),
+            vmem(tensors - 1, n_slots // 2, lanes),
             vmem(n_slots, low_width),
             vmem(n_slots, slice_width),
             vmem(n_slots, slice_width),
@@ -300,12 +356,13 @@
             vmem(tensors - 1, rows_dev, slice_width),
             pltpu.SemaphoreType.DMA,
             dma(base_chunks),
-            dma(halves),
+            dma(row_chunks),
             dma(expand_chunks),
-            *pairs(owners - 1),
+            *grids(owners - 1, row_chunks),
             *pairs(owners - 1),
             *pairs(tensors - 1),
-            *grids(tensors - 1, base_chunks),
+            *grids(2, base_chunks),
+            *pairs(base_chunks),
             *grids(owners - 1, expand_chunks),
             *grids(tensors - 1, expand_chunks),
         ],
@@ -331,7 +388,8 @@
     values = out_weight.size + shrink_weight.size + expand_weight.size
     values += rows * (features + 4 * width) + slots * (2 * features + low_width + 3 * slice_width)
     tiled = rows % (16 * tensors) == 0 and width % (8 * TILE) == 0 and slice_width % (4 * TILE) == 0
-    return tiled and features % TILE == 0 and 2 * values <= VMEM_LIMIT
+    tiled = tiled and tensors == 4 and features % (4 * TILE) == 0 and low_width % WIDE == 0
+    return tiled and 2 * values <= VMEM_LIMIT
 
 
 def plain(attended, out_weight, adapter_ids, shrink_weight, expand_weight):

time: 46.8 us -> 43.8 us (0.936)
  Pallas kernels: 44.8 us -> 41.8 us
    pallas_call x1, Pallas kernels: 44.8 us -> 41.8 us  [fused(): pl.pallas_call(functools.partial(fused_kernel, owners, tensors, base_chun...]
where the time goes in v2:
time: 43.8 us; the launch traced here: 43.6 us
  Pallas kernels  41.8 us (95%)
  other arithmetic  1.77 us (4%)
    pallas_call x1, Pallas kernels, fused(): pl.pallas_call(functools.partial(fused_kernel, owners, tensors, base_chun...  41.8 us
    broadcast_in_dim x1, other arithmetic, fused(): return summed.astype(BF16)[None]  1.77 us

profile of v2, /device:TPU:0, one launch (start us, length us, event | category | flops | bytes accessed | tf_op | source)
XLA Modules:
  0.0 43.6 jit_solution(7143645171171422268)
XLA Ops:
  0.0 41.8 %shard_map.55 = f32[16,8192]{1,0:T(8,128)} custom-call(s32[1,64]{1,0:T(1,128)} %ids_ref.1, bf16[64,2048]{1,0:T(8,128)(2,1)} %bitcast.9, bf16[2048,8192]{1,0:T(8,128)(2,1)} %w_hbm.1, bf16[2048,2048]{1,0:T(8,128)(2,1)} %bitcast.7, bf16[2048,2048]{1,0:T(8,128)(2,1)} %bitcast.8), custom_call_target="tpu_custom_call" | custom-call | tf_op jit(solution)/shard_map/pallas_call | solution.py:331
  41.8 1.8 %convert_bitcast_fusion = bf16[1,16,8192]{2,1,0:T(8,128)(2,1)} fusion(f32[16,8192]{1,0:T(8,128)} %shard_map.55), kind=kLoop, calls=%fused_computation | loop fusion | flops 131072 | bytes 786432 | tf_op jit(solution)/shard_map/broadcast_in_dim | solution.py:379

commit v3 on v2

--- a/solution.py
+++ b/solution.py
@@ -258,31 +258,21 @@
         load_e(c).start()
     base(0)
     base(1)
-    base(2)
-    base(3)
-    forward(0)
     for j in range(1, owners):
         send_ids(j).wait_recv()
     total = jnp.zeros((n_slots, lanes), F32)
     for k in range(row_chunks):
         total = shrink(k, total)
     send_total(total)
+    forward(0)
+    base(2)
+    base(3)
+    expand()
     forward(1)
-    base(4)
-    base(5)
-    base(6)
     forward(2)
-    expand()
-    base(7)
+    merge(0)
     forward(3)
-    forward(4)
-    forward(5)
-    merge(0)
-    forward(6)
     merge(1)
-    forward(7)
-    merge(2)
-    merge(3)
 
     for c in range(base_chunks):
         cols = pl.ds(c * chunk, chunk)
@@ -322,7 +312,7 @@
     adapters, rank, slice_width = expand_weight.shape
     low_width, lanes = adapters * rank, 2 * rank
     n_slots, rows_dev = owners * (rows // 2), rows // tensors
-    base_chunks, expand_chunks, row_chunks = 8, 4, 1
+    base_chunks, expand_chunks, row_chunks = 4, 2, 1
     dma = lambda *shape: pltpu.SemaphoreType.DMA(shape)
     pairs = lambda n: [dma(n), dma(n)]
     grids = lambda n, m: [dma(n, m), dma(n, m)]

time: 43.8 us -> 43.2 us (0.986)
  Pallas kernels: 41.8 us -> 41.3 us
    pallas_call x1, Pallas kernels: 41.8 us -> 41.3 us  [fused(): pl.pallas_call(functools.partial(fused_kernel, owners, tensors, base_chun...]
where the time goes in v3:
time: 43.2 us; the launch traced here: 43.1 us
  Pallas kernels  41.3 us (96%)
  other arithmetic  1.77 us (4%)
    pallas_call x1, Pallas kernels, fused(): pl.pallas_call(functools.partial(fused_kernel, owners, tensors, base_chun...  41.3 us
    broadcast_in_dim x1, other arithmetic, fused(): return summed.astype(BF16)[None]  1.77 us

profile of v3, /device:TPU:0, one launch (start us, length us, event | category | flops | bytes accessed | tf_op | source)
XLA Modules:
  0.0 43.1 jit_solution(10418630280689123040)
XLA Ops:
  0.0 41.3 %shard_map.55 = f32[16,8192]{1,0:T(8,128)} custom-call(s32[1,64]{1,0:T(1,128)} %ids_ref.1, bf16[64,2048]{1,0:T(8,128)(2,1)} %bitcast.9, bf16[2048,8192]{1,0:T(8,128)(2,1)} %w_hbm.1, bf16[2048,2048]{1,0:T(8,128)(2,1)} %bitcast.7, bf16[2048,2048]{1,0:T(8,128)(2,1)} %bitcast.8), custom_call_target="tpu_custom_call" | custom-call | tf_op jit(solution)/shard_map/pallas_call | solution.py:321
  41.3 1.8 %convert_bitcast_fusion = bf16[1,16,8192]{2,1,0:T(8,128)(2,1)} fusion(f32[16,8192]{1,0:T(8,128)} %shard_map.55), kind=kLoop, calls=%fused_computation | loop fusion | flops 131072 | bytes 786432 | tf_op jit(solution)/shard_map/broadcast_in_dim | solution.py:369
